TPU v7x, 32 devices: a whole 2x2x4 slice. The times are simulated.
32 devices in a mesh: dp: 4 (over z), pair: 8 (over y, x, core).
Axes of the slice: x: 2, y: 2, z: 4, core: 2. Of those that a mesh axis runs over, the one named last changes fastest.
Arguments:
- embeddings: bfloat16 [128, 512, 256], P('pair', 'dp'), may hold values from -6 to 6
- field_width: int32 [128], replicated, may hold values from 64 to 256, as said below
- pair_fields: int32 [384, 2], replicated, may hold values from 0 to 127, as said below
- pair_mats: bfloat16 [384, 256, 256], P('pair'), may hold values from -0.0048828125 to 0.0048828125
- labels: int32 [512], P('dp'), may hold values 0 or 1
Outputs:
- logits: float32 [512], P('dp')
- mat_grad: bfloat16 [384, 256, 256], P('pair', 'dp')
- emb_grad: float32 [128, 512, 256], P('pair', 'dp')
Inputs may be any that keep to these rules, and one draw needn't show every extreme that they name: `field_width`: each is 64, 128 or 256. `pair_fields`: the two fields of a pair differ. The 48 pairs of one owner read at most 3 different fields from the 16 fields of any one owner (field f is owned by index f // 16), and exactly 3 from some owner.
All inputs are finite; a program needn't handle non-finite values. No bound on the sum of `labels` on one device may be relied on, other than what follows from the above.
Results may differ from a plain program's by a relative error of at most 0.017.
Values may be sent and summed in bfloat16 or wider, within the bound.
No kernel may reach another device: no remote copies, remote signals or barrier semaphores. Data moves between devices by JAX's collectives and lax.ppermute only.
A program may use at most 128 MiB of HBM per device.

v0:
```python
import jax
import jax.numpy as jnp
from jax import lax
from jax.sharding import PartitionSpec as P

CAP = 3


def shards(embeddings, field_width, pair_fields, pair_mats, labels):
    owners = lax.axis_size("pair")
    owner_index = lax.axis_index("pair")
    field_count = embeddings.shape[0]
    sample_count = embeddings.shape[1]
    padded_width = embeddings.shape[2]
    pair_count = pair_mats.shape[0]
    column_ids = jnp.arange(padded_width, dtype=jnp.int32)
    width_mask = (column_ids[None, :] < field_width[:, None]).astype(jnp.bfloat16)
    own_mask = lax.dynamic_slice_in_dim(width_mask, owner_index * field_count, field_count, 0)
    masked = embeddings * own_mask[:, None, :]
    my_fields = owner_index * field_count + jnp.arange(field_count, dtype=jnp.int32)
    grouped = pair_fields.reshape(owners, pair_count * 2)
    needed = jnp.any(grouped[:, :, None] == my_fields[None, None, :], axis=1)
    slot_rank = jnp.cumsum(needed.astype(jnp.int32), axis=1) - 1
    slot_ids = jnp.arange(CAP, dtype=jnp.int32)
    selector = (needed[:, None, :] & (slot_rank[:, None, :] == slot_ids[None, :, None])).astype(
        jnp.bfloat16
    )
    outgoing = jnp.einsum("dcf,fsk->dcsk", selector, masked, preferred_element_type=jnp.bfloat16)
    incoming = lax.all_to_all(outgoing, "pair", split_axis=0, concat_axis=0, tiled=True)
    received = incoming.reshape(owners * CAP, sample_count, padded_width)
    my_pairs = lax.dynamic_slice_in_dim(pair_fields, owner_index * pair_count, pair_count, 0)
    every_field = jnp.arange(owners * field_count, dtype=jnp.int32)
    wanted = jnp.any(my_pairs.reshape(-1)[:, None] == every_field[None, :], axis=0).reshape(
        owners, field_count
    )
    slot_table = (jnp.cumsum(wanted.astype(jnp.int32), axis=1) - 1).reshape(-1)
    slot_index = my_pairs // field_count * CAP + slot_table[my_pairs]
    left_rows = received[slot_index[:, 0]]
    right_rows = received[slot_index[:, 1]]
    projected = jnp.einsum("psk,pkl->psl", left_rows, pair_mats, preferred_element_type=jnp.float32)
    partial_value = jnp.sum(projected * right_rows, axis=(0, 2))
    logits = lax.psum(partial_value, "pair")
    grad_out = jax.nn.sigmoid(logits) - labels.astype(jnp.float32)
    toward_left = grad_out[None, :, None] * jnp.einsum(
        "psl,pkl->psk", right_rows, pair_mats, preferred_element_type=jnp.float32
    )
    toward_right = grad_out[None, :, None] * projected
    slot_grads = jnp.zeros((owners * CAP, sample_count, padded_width), jnp.float32)
    slot_grads = (
        slot_grads.at[slot_index[:, 0]].add(toward_left).at[slot_index[:, 1]].add(toward_right)
    )
    slot_grads = slot_grads.astype(jnp.bfloat16).reshape(owners, CAP, sample_count, padded_width)
    returned = lax.all_to_all(slot_grads, "pair", split_axis=0, concat_axis=0, tiled=True)
    emb_grad = jnp.einsum("dcf,dcsk->fsk", selector, returned, preferred_element_type=jnp.float32)
    emb_grad = emb_grad * own_mask[:, None, :].astype(jnp.float32)
    scaled = (grad_out[None, :, None] * left_rows).astype(jnp.bfloat16)
    mat_term = jnp.einsum("psk,psl->pkl", scaled, right_rows, preferred_element_type=jnp.float32)
    mat_grad = lax.psum_scatter(
        mat_term.astype(jnp.bfloat16), "dp", scatter_dimension=1, tiled=True
    )
    return (logits, mat_grad, emb_grad)


def solution(mesh):
    in_specs = (P("pair", "dp", None), P(), P(), P("pair", None, None), P("dp"))
    out_specs = (P("dp"), P("pair", "dp", None), P("pair", "dp", None))
    return jax.shard_map(shards, mesh=mesh, in_specs=in_specs, out_specs=out_specs, check_vma=False)
```

profile of v0, /device:TPU:0, one launch (start us, length us, event | category | flops | bytes accessed | tf_op | source)
XLA Modules:
  0.0 190.4 jit_solution(742963178127088369)
XLA Ops:
  7.2 0.7 dynamic-slice
  8.0 0.8 copy.34
  9.0 0.3 compare_reduce_fusion
  9.4 1.3 broadcast_multiply_fusion.2
  10.7 0.7 fusion.2
  11.5 1.5 copy.36
  13.0 5.2 %all-to-all-start = ((bf16[8,3,128,256]{3,2,1,0:T(8,128)(2,1)}), bf16[8,3,128,256]{3,2,1,0:T(8,128)(2,1)S(1)}, u32[]{:S(2)}, u32[]{:S(2)}) async-start(bf16[8,3,128,256]{3,2,1,0:T(8,128)(2,1)} %copy.36), calls=%async_computation | async-start | bytes 3145728 | tf_op jit(solution)/shard_map/all_to_all | solution.py:29
  18.9 1.2 gather_fusion
  20.5 18.7 %all-to-all-done = bf16[8,3,128,256]{3,2,1,0:T(8,128)(2,1)S(1)} async-done(((bf16[8,3,128,256]{3,2,1,0:T(8,128)(2,1)}), bf16[8,3,128,256]{3,2,1,0:T(8,128)(2,1)S(1)}, u32[]{:S(2)}, u32[]{:S(2)}) %all-to-all-start) | async-done | bytes 1572896 | tf_op jit(solution)/shard_map/all_to_all | solution.py:29
  39.2 1.1 copy-done
  40.3 2.2 %gather_fusion.2 = bf16[48,128,256]{2,1,0:T(8,128)(2,1)S(1)} fusion(bf16[24,128,256]{2,1,0:T(8,128)(2,1)} %bitcast.20, s32[1024]{0:T(1024)S(1)} %get-tuple-element.26), kind=kCustom, calls=%fused_computation.2 | custom fusion | bytes 6291648 | tf_op jit(solution)/shard_map/gather | solution.py:39
  42.5 3.9 %gather_fusion.1 = bf16[48,128,256]{2,1,0:T(8,128)(2,1)} fusion(bf16[24,128,256]{2,1,0:T(8,128)(2,1)} %bitcast.21, s32[1024]{0:T(1024)S(1)} %get-tuple-element.27), kind=kCustom, calls=%fused_computation.1 | custom fusion | bytes 6291648 | tf_op jit(solution)/shard_map/gather | solution.py:38
  46.4 7.4 %multiply_reduce_fusion = (f32[128]{0:T(128)S(1)}, f32[48,128,256]{2,1,0:T(8,128)}) fusion(bf16[48,128,256]{2,1,0:T(8,128)(2,1)S(1)} %gather_fusion.2, bf16[48,128,256]{2,1,0:T(8,128)(2,1)} %gather_fusion.1, bf16[48,256,256]{2,1,0:T(8,128)(2,1)} %param.8), kind=kOutput, calls=%fused_computation.6 | convolution fusion | flops 810024832 | bytes 18874880 | tf_op jit(solution)/shard_map/psk,pkl->psl/dot_general | solution.py:40
  53.8 11.8 %psum.7 = f32[128]{0:T(128)S(1)} all-reduce(f32[128]{0:T(128)S(1)} %get-tuple-element.24), channel_id=1, replica_groups=mesh['dp'=4,'pair'=8] {'pair'}, use_global_device_ids=true, to_apply=%region_5.6 | all-reduce | flops 128 | bytes 1024 | tf_op jit(solution)/shard_map/psum | solution.py:42
  65.6 6.5 %convolution_convert_fusion = bf16[48,256,256]{2,1,0:T(8,128)(2,1)} fusion(bf16[48,128,256]{2,1,0:T(8,128)(2,1)S(1)} %gather_fusion.2, bf16[48,128,256]{2,1,0:T(8,128)(2,1)} %gather_fusion.1, f32[128]{0:T(128)S(1)} %divide_subtract_fusion), kind=kOutput, calls=%fused_computation.7 | convolution fusion | flops 813170688 | bytes 12583424 | tf_op jit(solution)/shard_map/psk,psl->pkl/dot_general | solution.py:57
  72.2 8.2 %broadcast_multiply_fusion.1 = f32[48,128,256]{2,1,0:T(8,128)} fusion(f32[128]{0:T(128)S(1)} %divide_subtract_fusion, bf16[48,128,256]{2,1,0:T(8,128)(2,1)S(1)} %gather_fusion.2, bf16[48,256,256]{2,1,0:T(8,128)(2,1)} %param.8), kind=kOutput, calls=%fused_computation.9 | convolution fusion | flops 806879232 | bytes 15729152 | tf_op jit(solution)/shard_map/psl,pkl->psk/dot_general | solution.py:44
  80.4 0.3 broadcast_in_dim.5
  80.8 9.5 %scatter_fusion = f32[24,128,256]{2,1,0:T(8,128)S(1)} fusion(f32[24,128,256]{2,1,0:T(8,128)S(1)} %broadcast_in_dim.5, s32[48]{0:T(128)S(1)} %get-tuple-element.19, f32[48,128,256]{2,1,0:T(8,128)} %broadcast_multiply_fusion.1), kind=kCustom, calls=%fused_computation.3 | custom fusion | flops 1572864 | bytes 18874560 | tf_op jit(solution)/shard_map/scatter-add | solution.py:50
  90.3 6.5 %broadcast_multiply_fusion = f32[48,128,256]{2,1,0:T(8,128)} fusion(f32[48,128,256]{2,1,0:T(8,128)} %get-tuple-element.25, f32[128]{0:T(128)S(1)} %divide_subtract_fusion), kind=kLoop, calls=%fused_computation.8 | loop fusion | flops 1572864 | bytes 12583424 | tf_op jit(solution)/shard_map/mul | solution.py:47
  96.8 9.5 %scatter_fusion.1 = f32[24,128,256]{2,1,0:T(8,128)S(1)} fusion(f32[24,128,256]{2,1,0:T(8,128)S(1)} %scatter_fusion, s32[48]{0:T(128)S(1)} %get-tuple-element.18, f32[48,128,256]{2,1,0:T(8,128)} %broadcast_multiply_fusion), kind=kCustom, calls=%fused_computation.4 | custom fusion | flops 1572864 | bytes 18874560 | tf_op jit(solution)/shard_map/scatter-add | solution.py:50
  106.5 23.7 %all_to_all.10 = bf16[8,3,128,256]{3,2,1,0:T(8,128)(2,1)S(1)} all-to-all(bf16[8,3,128,256]{3,2,1,0:T(8,128)(2,1)S(1)} %bitcast.22), channel_id=1, replica_groups=mesh['dp'=4,'pair'=8] {'pair'}, dimensions={0} | all-to-all | bytes 3145728 | tf_op jit(solution)/shard_map/all_to_all | solution.py:53
  130.1 1.0 bitcast_multiply_fusion
  131.1 2.5 %copy.40 = f32[16,128,256]{2,1,0:T(8,128)} copy(f32[16,128,256]{2,0,1:T(8,128)S(1)} %bitcast_multiply_fusion) | data formatting | bytes 4194304
  133.7 49.9 %reduce-scatter.2.cloned.1.call-done = bf16[48,64,256]{2,1,0:T(8,128)(2,1)} async-done(((bf16[48,256,256]{2,1,0:T(8,128)(2,1)}), bf16[48,64,256]{2,1,0:T(8,128)(2,1)}) %reduce-scatter.2.cloned.1.call-update) | async-done | bytes 1572880 | tf_op jit(solution)/shard_map/reduce_scatter | solution.py:58
  (29 shorter events, 1.7 us)
Async XLA Ops:
  13.0 26.2 %all-to-all-start = ((bf16[8,3,128,256]{3,2,1,0:T(8,128)(2,1)}), bf16[8,3,128,256]{3,2,1,0:T(8,128)(2,1)S(1)}, u32[]{:S(2)}, u32[]{:S(2)}) async-start(bf16[8,3,128,256]{3,2,1,0:T(8,128)(2,1)} %copy.36), calls=%async_computation | async-start | bytes 3145728 | tf_op jit(solution)/shard_map/all_to_all | solution.py:29
  18.2 165.4 %reduce-scatter.2.cloned.1.call-start = ((), (), s32[]{:S(2)}) async-start(), calls=%async_computation.3 | async-start | bytes 7864320 | tf_op jit(solution)/shard_map/reduce_scatter | solution.py:58
  39.2 1.1 copy-start
  46.4 19.2 %copy-start.1 = (s32[128]{0:T(128)S(1)}, s32[128]{0:T(128)}, u32[]{:S(2)}) copy-start(s32[128]{0:T(128)} %param.9) | copy-start | bytes 1540
  65.6 6.6 %copy-start.2 = (f32[128]{0:T(128)}, f32[128]{0:T(128)S(1)}, u32[]{:S(2)}) copy-start(f32[128]{0:T(128)S(1)} %psum.7) | copy-start | bytes 1540
Sparse Core Ops, SparseCore 0:
  72.3 111.1 reduce-scatter.1
where the time goes:
time: 191 us; the launch traced here: 190 us
  waiting for transfers between devices  68.6 us (36%)
  blocking collectives  35.4 us (19%)
  other arithmetic  28 us (15%)
  matrix products  23.9 us (13%)
  local copies, waits for them, and re-layouts  15 us (8%)
  between operations  14.2 us (7%)
  starting transfers between devices  5.21 us (3%)
    reduce_scatter x1, waiting for transfers between devices, shards(): lax.psum_scatter(mat_term.astype(jnp.bfloat16), 'dp', scatter_dimension=1...  49.9 us
    all_to_all x1, blocking collectives, shards(): lax.all_to_all(slot_grads, 'pair', split_axis=0, concat_axis=0, tiled=True)  23.7 us
    scatter-add x2, other arithmetic, shards(): slot_grads.at[slot_index[:, 0]].add(toward_left).at[slot_index[:, 1]]  19 us
    all_to_all x1, waiting for transfers between devices, shards(): lax.all_to_all(outgoing, 'pair', split_axis=0, concat_axis=0, tiled=True)  18.7 us
    psum x1, blocking collectives, shards(): logits = lax.psum(partial_value, 'pair')  11.8 us
    dot_general x1, matrix products, shards(): jnp.einsum('psl,pkl->psk', right_rows, pair_mats, preferred_element_type=...  8.23 us
    dot_general x1, matrix products, shards(): jnp.einsum('psk,pkl->psl', left_rows, pair_mats, preferred_element_type=j...  7.41 us
    dot_general x1, matrix products, shards(): jnp.einsum('psk,psl->pkl', scaled, right_rows, preferred_element_type=jnp...  6.53 us
  transfers between devices with their start and end apart: 2, of which 2 were waited for; matrix products, arithmetic and copies ran while one was open for 21% of the time, Pallas kernels for 0%

commit v1 on v0

--- a/solution.py
+++ b/solution.py
@@ -39,7 +39,9 @@
     right_rows = received[slot_index[:, 1]]
     projected = jnp.einsum("psk,pkl->psl", left_rows, pair_mats, preferred_element_type=jnp.float32)
     partial_value = jnp.sum(projected * right_rows, axis=(0, 2))
-    logits = lax.psum(partial_value, "pair")
+    logits = partial_value
+    for hop in (1, 2, 4):
+        logits = logits + lax.ppermute(logits, "pair", [(dev, dev ^ hop) for dev in range(8)])
     grad_out = jax.nn.sigmoid(logits) - labels.astype(jnp.float32)
     toward_left = grad_out[None, :, None] * jnp.einsum(
         "psl,pkl->psk", right_rows, pair_mats, preferred_element_type=jnp.float32

time: 191 us -> 185 us (0.969)
  blocking collectives: 35.4 us -> 23.4 us
  waiting for transfers between devices: 68.6 us -> 75.2 us
    psum x1 -> x0, blocking collectives: 11.8 us -> none  [shards(): logits = lax.psum(partial_value, 'pair')]
    ppermute x0 -> x3, waiting for transfers between devices: none -> 7.13 us  [shards(): lax.ppermute(logits, 'pair', [(dev, dev ^ hop) for dev in range(8)])]
  transfers between devices with their start and end apart: 2 -> 5, of which waited for: 2 -> 5; matrix products, arithmetic and copies ran while one was open for 21% -> 21% of each run, Pallas kernels for 0% -> 0%
where the time goes in v1:
time: 185 us
  waiting for transfers between devices  75.2 us (41%)
  other arithmetic  28.5 us (15%)
  blocking collectives  23.4 us (13%)
  matrix products  22 us (12%)
  local copies, waits for them, and re-layouts  15.1 us (8%)
  between operations  14.2 us (8%)
  starting transfers between devices  6.28 us (3%)
    reduce_scatter x1, waiting for transfers between devices, shards(): lax.psum_scatter(mat_term.astype(jnp.bfloat16), 'dp', scatter_dimension=1...  49.4 us
    all_to_all x1, blocking collectives, shards(): lax.all_to_all(slot_grads, 'pair', split_axis=0, concat_axis=0, tiled=True)  23.4 us
    scatter-add x2, other arithmetic, shards(): slot_grads.at[slot_index[:, 0]].add(toward_left).at[slot_index[:, 1]]  19 us
    all_to_all x1, waiting for transfers between devices, shards(): lax.all_to_all(outgoing, 'pair', split_axis=0, concat_axis=0, tiled=True)  18.7 us
    dot_general x1, matrix products, shards(): jnp.einsum('psl,pkl->psk', right_rows, pair_mats, preferred_element_type=...  7.97 us
    dot_general x1, matrix products, shards(): jnp.einsum('psk,pkl->psl', left_rows, pair_mats, preferred_element_type=j...  7.54 us
    ppermute x3, waiting for transfers between devices, shards(): lax.ppermute(logits, 'pair', [(dev, dev ^ hop) for dev in range(8)])  7.13 us
    mul x1, other arithmetic, shards(): toward_right = grad_out[None, :, None] * projected  6.36 us
  transfers between devices with their start and end apart: 5, of which 5 were waited for; matrix products, arithmetic and copies ran while one was open for 21% of the time, Pallas kernels for 0%

profile of v1, /device:TPU:0, one launch (start us, length us, event | category | flops | bytes accessed | tf_op | source)
XLA Modules:
  0.0 184.7 jit_solution(2902397970083209178)
XLA Ops:
  7.2 0.7 dynamic-slice
  8.0 0.8 copy.34
  9.4 1.3 broadcast_multiply_fusion.2
  10.7 0.7 fusion.2
  11.5 1.5 copy.36
  13.0 5.2 %all-to-all-start = ((bf16[8,3,128,256]{3,2,1,0:T(8,128)(2,1)}), bf16[8,3,128,256]{3,2,1,0:T(8,128)(2,1)S(1)}, u32[]{:S(2)}, u32[]{:S(2)}) async-start(bf16[8,3,128,256]{3,2,1,0:T(8,128)(2,1)} %copy.36), calls=%async_computation | async-start | bytes 3145728 | tf_op jit(solution)/shard_map/all_to_all | solution.py:29
  18.9 1.2 gather_fusion
  20.5 18.7 %all-to-all-done = bf16[8,3,128,256]{3,2,1,0:T(8,128)(2,1)S(1)} async-done(((bf16[8,3,128,256]{3,2,1,0:T(8,128)(2,1)}), bf16[8,3,128,256]{3,2,1,0:T(8,128)(2,1)S(1)}, u32[]{:S(2)}, u32[]{:S(2)}) %all-to-all-start) | async-done | bytes 1572896 | tf_op jit(solution)/shard_map/all_to_all | solution.py:29
  39.2 1.1 copy-done
  40.3 2.2 %gather_fusion.2 = bf16[48,128,256]{2,1,0:T(8,128)(2,1)S(1)} fusion(bf16[24,128,256]{2,1,0:T(8,128)(2,1)} %bitcast.20, s32[1024]{0:T(1024)S(1)} %get-tuple-element.28), kind=kCustom, calls=%fused_computation.2 | custom fusion | bytes 6291648 | tf_op jit(solution)/shard_map/gather | solution.py:39
  42.5 4.0 %gather_fusion.1 = bf16[48,128,256]{2,1,0:T(8,128)(2,1)} fusion(bf16[24,128,256]{2,1,0:T(8,128)(2,1)} %bitcast.21, s32[1024]{0:T(1024)S(1)} %get-tuple-element.29), kind=kCustom, calls=%fused_computation.1 | custom fusion | bytes 6291648 | tf_op jit(solution)/shard_map/gather | solution.py:38
  46.5 7.5 %multiply_reduce_fusion = (f32[128]{0:T(128)S(1)}, f32[48,128,256]{2,1,0:T(8,128)}) fusion(bf16[48,128,256]{2,1,0:T(8,128)(2,1)S(1)} %gather_fusion.2, bf16[48,128,256]{2,1,0:T(8,128)(2,1)} %gather_fusion.1, bf16[48,256,256]{2,1,0:T(8,128)(2,1)} %param.8), kind=kOutput, calls=%fused_computation.6 | convolution fusion | flops 810024832 | bytes 18874880 | tf_op jit(solution)/shard_map/psk,pkl->psl/dot_general | solution.py:40
  54.0 1.1 collective-permute-done
  55.6 3.0 %collective-permute-done.1 = f32[128]{0:T(128)S(1)} collective-permute-done((f32[128]{0:T(128)S(1)}, f32[128]{0:T(128)S(1)}, u32[]{:S(2)}, u32[]{:S(2)}) %collective-permute-start.1) | collective-permute-done | bytes 544 | tf_op jit(solution)/shard_map/ppermute | solution.py:44
  59.2 3.0 %collective-permute-done.2 = f32[128]{0:T(128)S(1)} collective-permute-done((f32[128]{0:T(128)S(1)}, f32[128]{0:T(128)S(1)}, u32[]{:S(2)}, u32[]{:S(2)}) %collective-permute-start.2) | collective-permute-done | bytes 544 | tf_op jit(solution)/shard_map/ppermute | solution.py:44
  62.7 4.8 %convolution_convert_fusion = bf16[48,256,256]{2,1,0:T(8,128)(2,1)} fusion(bf16[48,128,256]{2,1,0:T(8,128)(2,1)S(1)} %gather_fusion.2, bf16[48,128,256]{2,1,0:T(8,128)(2,1)S(1)} %copy-done.1, f32[128]{0:T(128)S(1)} %get-tuple-element.20), kind=kOutput, calls=%fused_computation.7 | convolution fusion | flops 813170688 | bytes 12583424 | tf_op jit(solution)/shard_map/psk,psl->pkl/dot_general | solution.py:59
  67.5 8.0 %broadcast_multiply_fusion.1 = f32[48,128,256]{2,1,0:T(8,128)} fusion(f32[128]{0:T(128)S(1)} %get-tuple-element.20, bf16[48,128,256]{2,1,0:T(8,128)(2,1)S(1)} %gather_fusion.2, bf16[48,256,256]{2,1,0:T(8,128)(2,1)} %param.8), kind=kOutput, calls=%fused_computation.9 | convolution fusion | flops 806879232 | bytes 15729152 | tf_op jit(solution)/shard_map/psl,pkl->psk/dot_general | solution.py:46
  75.8 9.5 %scatter_fusion = f32[24,128,256]{2,1,0:T(8,128)S(1)} fusion(f32[24,128,256]{2,1,0:T(8,128)S(1)} %broadcast_in_dim.5, s32[48]{0:T(128)S(1)} %get-tuple-element.19, f32[48,128,256]{2,1,0:T(8,128)} %broadcast_multiply_fusion.1), kind=kCustom, calls=%fused_computation.3 | custom fusion | flops 1572864 | bytes 18874560 | tf_op jit(solution)/shard_map/scatter-add | solution.py:52
  85.4 6.4 %broadcast_multiply_fusion = f32[48,128,256]{2,1,0:T(8,128)} fusion(f32[48,128,256]{2,1,0:T(8,128)} %get-tuple-element.27, f32[128]{0:T(128)S(1)} %get-tuple-element.20), kind=kLoop, calls=%fused_computation.8 | loop fusion | flops 1572864 | bytes 12583424 | tf_op jit(solution)/shard_map/mul | solution.py:49
  91.8 9.5 %scatter_fusion.1 = f32[24,128,256]{2,1,0:T(8,128)S(1)} fusion(f32[24,128,256]{2,1,0:T(8,128)S(1)} %scatter_fusion, s32[48]{0:T(128)S(1)} %get-tuple-element.18, f32[48,128,256]{2,1,0:T(8,128)} %broadcast_multiply_fusion), kind=kCustom, calls=%fused_computation.4 | custom fusion | flops 1572864 | bytes 18874560 | tf_op jit(solution)/shard_map/scatter-add | solution.py:52
  101.5 23.4 %all_to_all.10 = bf16[8,3,128,256]{3,2,1,0:T(8,128)(2,1)S(1)} all-to-all(bf16[8,3,128,256]{3,2,1,0:T(8,128)(2,1)S(1)} %bitcast.22), channel_id=1, replica_groups=mesh['dp'=4,'pair'=8] {'pair'}, dimensions={0} | all-to-all | bytes 3145728 | tf_op jit(solution)/shard_map/all_to_all | solution.py:55
  124.9 1.0 bitcast_multiply_fusion
  125.9 2.5 %copy.40 = f32[16,128,256]{2,1,0:T(8,128)} copy(f32[16,128,256]{2,0,1:T(8,128)S(1)} %bitcast_multiply_fusion) | data formatting | bytes 4194304
  128.4 49.4 %reduce-scatter.2.cloned.1.call-done = bf16[48,64,256]{2,1,0:T(8,128)(2,1)} async-done(((bf16[48,256,256]{2,1,0:T(8,128)(2,1)}), bf16[48,64,256]{2,1,0:T(8,128)(2,1)}) %reduce-scatter.2.cloned.1.call-update) | async-done | bytes 1572880 | tf_op jit(solution)/shard_map/reduce_scatter | solution.py:60
  (36 shorter events, 3.9 us)
Async XLA Ops:
  13.0 26.2 %all-to-all-start = ((bf16[8,3,128,256]{3,2,1,0:T(8,128)(2,1)}), bf16[8,3,128,256]{3,2,1,0:T(8,128)(2,1)S(1)}, u32[]{:S(2)}, u32[]{:S(2)}) async-start(bf16[8,3,128,256]{3,2,1,0:T(8,128)(2,1)} %copy.36), calls=%async_computation | async-start | bytes 3145728 | tf_op jit(solution)/shard_map/all_to_all | solution.py:29
  18.2 159.7 %reduce-scatter.2.cloned.1.call-start = ((), (), s32[]{:S(2)}) async-start(), calls=%async_computation.3 | async-start | bytes 7864320 | tf_op jit(solution)/shard_map/reduce_scatter | solution.py:60
  39.2 1.1 copy-start
  46.4 15.8 %copy-start.2 = (s32[128]{0:T(128)S(1)}, s32[128]{0:T(128)}, u32[]{:S(2)}) copy-start(s32[128]{0:T(128)} %param.9) | copy-start | bytes 1540
  46.4 16.3 %copy-start.1 = (bf16[48,128,256]{2,1,0:T(8,128)(2,1)S(1)}, bf16[48,128,256]{2,1,0:T(8,128)(2,1)}, u32[]{:S(2)}) copy-start(bf16[48,128,256]{2,1,0:T(8,128)(2,1)} %gather_fusion.1) | copy-start | bytes 9437188
  54.0 1.1 collective-permute-start
  55.1 3.5 %collective-permute-start.1 = (f32[128]{0:T(128)S(1)}, f32[128]{0:T(128)S(1)}, u32[]{:S(2)}, u32[]{:S(2)}) collective-permute-start(f32[128]{0:T(128)S(1)} %add.71), channel_id=1, source_target_pairs={{0,2},{1,3},{2,0},{3,1},{4,6},{5,7},{6,4},{7,5},{8,10},{9,11},{10,... | collective-permute-start | bytes 1544 | tf_op jit(solution)/shard_map/ppermute | solution.py:44
  58.7 3.5 %collective-permute-start.2 = (f32[128]{0:T(128)S(1)}, f32[128]{0:T(128)S(1)}, u32[]{:S(2)}, u32[]{:S(2)}) collective-permute-start(f32[128]{0:T(128)S(1)} %add.72), channel_id=1, source_target_pairs={{0,4},{1,5},{2,6},{3,7},{4,0},{5,1},{6,2},{7,3},{8,12},{9,13},{10,... | collective-permute-start | bytes 1544 | tf_op jit(solution)/shard_map/ppermute | solution.py:44
Sparse Core Ops, SparseCore 0:
  67.7 110.1 reduce-scatter.1
